TPU v7x, 32 devices: a whole 2x2x4 slice. The times are simulated.
32 devices in a mesh: dom: 8 (over z, x), wide: 4 (over y, core).
Axes of the slice: x: 2, y: 2, z: 4, core: 2. Of those that a mesh axis runs over, the one named last changes fastest.
Arguments:
- features: bfloat16 [8192, 512], P(('dom', 'wide')), may hold values from -6 to 6
- w_self: bfloat16 [512, 512], replicated, may hold values from -0.25 to 0.25
- w_neigh: bfloat16 [512, 512], replicated, may hold values from -0.25 to 0.25
- boundary: int32 [32, 2, 64], P(('dom', 'wide')), may hold values from 0 to 255
- neighbors: int32 [8192, 16], P(('dom', 'wide')), may hold values from 0 to 384, as said below
- anchors: int32 [128, 32], P(('dom', 'wide')), may hold values from 0 to 255
- negatives: int32 [128, 32, 8], P(('dom', 'wide')), may hold values from 0 to 255
- positives: int32 [8192, 2], P(('dom', 'wide')), may hold values from 0 to 255
Outputs:
- embed: bfloat16 [8192, 512], P(('dom', 'wide'))
- embed_grad: bfloat16 [8192, 512], P(('dom', 'wide'))
Inputs may be any that keep to these rules, and one draw needn't show every extreme that they name: `neighbors`: each row has its live slots first, 1 to 16 of them; the first node of every partition has 16; slots after the live ones hold 384. `anchors`: rows of the own partition. `negatives`: rows of the own partition. `positives`: rows of the own partition.
All inputs are finite; a program needn't handle non-finite values.
Results may differ from a plain program's by a relative error of at most 0.0053.
Values may be sent and summed in bfloat16 or wider, within the bound.
A program may use at most 64 MiB of HBM per device.

v0:
```python
import math

import jax
import jax.numpy as jnp
from jax import lax
from jax.sharding import PartitionSpec as P


def passed_along(block, axis, distance):
    devices = range(lax.axis_size(axis))
    route = [(i - distance, i) for i in devices if i - distance in devices]
    return lax.ppermute(block, axis, route)


def pick_rows(index, table):
    columns = jnp.arange(table.shape[0], dtype=jnp.int32)[None, :]
    onehot = (index.reshape(-1)[:, None] == columns).astype(table.dtype)
    return jnp.dot(onehot, table, preferred_element_type=jnp.float32).astype(table.dtype)


def spread_rows(index, weights, rows, node_dev):
    nodes = jnp.arange(node_dev, dtype=jnp.int32)[:, None]
    mixing = jnp.where(nodes == index.reshape(-1)[None, :], weights[None, :], 0.0)
    return jnp.dot(
        mixing,
        rows.astype(jnp.float32),
        precision=lax.Precision.HIGHEST,
        preferred_element_type=jnp.float32,
    )


def body(features, w_self, w_neigh, boundary, neighbors, anchors, negatives, positives):
    node_dev = features.shape[0]
    width = features.shape[1]
    scale = 1.0 / math.sqrt(width)
    lists = boundary[0]
    below = passed_along(pick_rows(lists[0], features), "dom", 1)
    above = passed_along(pick_rows(lists[1], features), "dom", -1)
    table = jnp.concatenate([features, below, above], axis=0)
    table_rows = table.shape[0]
    columns = jnp.arange(table_rows, dtype=jnp.int32)[None, :]
    counts = jnp.zeros((node_dev, table_rows), jnp.bfloat16)
    for slot in range(neighbors.shape[1]):
        counts = counts + (neighbors[:, slot : slot + 1] == columns).astype(jnp.bfloat16)
    degree = jnp.sum((neighbors < table_rows).astype(jnp.float32), axis=1)
    summed = jnp.dot(counts, table, preferred_element_type=jnp.float32)
    mean = (summed / degree[:, None]).astype(jnp.bfloat16)
    embed = (
        jnp.dot(features, w_self, preferred_element_type=jnp.float32)
        + jnp.dot(mean, w_neigh, preferred_element_type=jnp.float32)
    ).astype(jnp.bfloat16)
    peers = anchors.shape[0]
    anch = anchors.shape[1]
    fan = negatives.shape[2]
    a_rows = pick_rows(anchors, embed).reshape(peers, anch, width)
    own_rows = pick_rows(negatives, embed).reshape(peers, anch, fan, width)
    got = lax.all_to_all(a_rows, "wide", split_axis=0, concat_axis=0, tiled=True)
    coef = jax.nn.sigmoid(
        jnp.einsum("vad,vakd->vak", got, own_rows, preferred_element_type=jnp.float32) * scale
    )
    nodes = jnp.arange(node_dev, dtype=jnp.int32)[:, None, None]
    mixing = jnp.sum(
        jnp.where(
            nodes == negatives.reshape(1, peers * anch, fan),
            coef.reshape(1, peers * anch, fan),
            0.0,
        ),
        axis=2,
    )
    grad = jnp.dot(
        mixing,
        got.reshape(-1, width).astype(jnp.float32),
        precision=lax.Precision.HIGHEST,
        preferred_element_type=jnp.float32,
    )
    back = jnp.sum(coef[..., None] * own_rows.astype(jnp.float32), axis=2)
    anchor_terms = lax.all_to_all(back, "wide", split_axis=0, concat_axis=0, tiled=True)
    ones = jnp.ones((peers * anch,), jnp.float32)
    grad = grad + spread_rows(anchors, ones, anchor_terms.reshape(-1, width), node_dev)
    first = pick_rows(positives[:, 0], embed)
    second = pick_rows(positives[:, 1], embed)
    coef_pos = (
        jax.nn.sigmoid(
            jnp.einsum("nd,nd->n", first, second, preferred_element_type=jnp.float32) * scale
        )
        - 1.0
    )
    both_index = jnp.concatenate([positives[:, 0], positives[:, 1]], axis=0)
    both_coef = jnp.concatenate([coef_pos, coef_pos], axis=0)
    both_rows = jnp.concatenate([second, first], axis=0)
    grad = grad + spread_rows(both_index, both_coef, both_rows, node_dev)
    return (embed, grad.astype(jnp.bfloat16))


def solution(mesh):
    return jax.shard_map(
        body,
        mesh=mesh,
        in_specs=(
            P(("dom", "wide"), None),
            P(),
            P(),
            P(("dom", "wide"), None, None),
            P(("dom", "wide"), None),
            P(("dom", "wide"), None),
            P(("dom", "wide"), None, None),
            P(("dom", "wide"), None),
        ),
        out_specs=(P(("dom", "wide"), None), P(("dom", "wide"), None)),
        check_vma=False,
    )
```

profile of v0, /device:TPU:24, one launch (start us, length us, event | category | flops | bytes accessed | tf_op | source)
XLA Modules:
  0.0 40.1 jit_solution(15722475040783173711)
XLA Ops:
  0.6 0.8 %slice_bitcast_fusion.1 = (s32[64]{0:T(128)S(1)}, s32[64]{0:T(128)S(1)}) fusion(s32[1,2,64]{2,1,0:T(2,128)} %param.11), kind=kLoop, calls=%fused_computation.125 | loop fusion | bytes 1024 | tf_op jit(solution)/shard_map/eq | solution.py:17
  1.4 1.2 %convolution_convert_fusion.5 = bf16[64,512]{1,0:T(8,128)(2,1)S(1)} fusion(bf16[256,512]{1,0:T(8,128)(2,1)} %param.8, s32[64]{0:T(128)S(1)} %get-tuple-element.20), kind=kOutput, calls=%fused_computation.13 | convolution fusion | flops 16826368 | bytes 327936 | tf_op jit(solution)/shard_map/dot_general | solution.py:18
  2.6 3.5 %collective-permute-start = (bf16[64,512]{1,0:T(8,128)(2,1)S(1)}, bf16[64,512]{1,0:T(8,128)(2,1)S(1)}, u32[]{:S(2)}, u32[]{:S(2)}) collective-permute-start(bf16[64,512]{1,0:T(8,128)(2,1)S(1)} %convolution_convert_fusion.5), channel_id=1, source_target_pairs={{0,4},{4,8},{8,12},{12,16},{16,20},{20,24},{24,28},{1,5},{5,9},{9,... | collective-permute-start | bytes 196616 | tf_op jit(solution)/shard_map/ppermute | solution.py:12
  6.1 1.2 %convolution_convert_fusion.4 = bf16[64,512]{1,0:T(8,128)(2,1)S(1)} fusion(bf16[256,512]{1,0:T(8,128)(2,1)} %param.8, s32[64]{0:T(128)S(1)} %get-tuple-element.21), kind=kOutput, calls=%fused_computation.12 | convolution fusion | flops 16826368 | bytes 327936 | tf_op jit(solution)/shard_map/dot_general | solution.py:18
  7.3 3.3 %collective-permute-start.1 = (bf16[64,512]{1,0:T(8,128)(2,1)S(1)}, bf16[64,512]{1,0:T(8,128)(2,1)S(1)}, u32[]{:S(2)}, u32[]{:S(2)}) collective-permute-start(bf16[64,512]{1,0:T(8,128)(2,1)S(1)} %convolution_convert_fusion.4), channel_id=1, source_target_pairs={{4,0},{8,4},{12,8},{16,12},{20,16},{24,20},{28,24},{5,1},{9,5},{13... | collective-permute-start | bytes 196616 | tf_op jit(solution)/shard_map/ppermute | solution.py:12
  10.7 1.0 %fusion.140 = (s32[256,1]{0,1:T(1,128)S(1)}, s32[256,1]{0,1:T(1,128)S(1)}, s32[256,1]{0,1:T(1,128)S(1)}, s32[256,1]{0,1:T(1,128)S(1)}, s32[256,1]{0,1:T(1,128)S(...) fusion(s32[256,16]{0,1:T(8,128)} %param.12), kind=kLoop, calls=%fused_computation.131 | loop fusion | bytes 32768 | tf_op jit(solution)/shard_map/slice | solution.py:44
  11.7 0.7 %convert_reduce_fusion = f32[256]{0:T(256)S(1)} fusion(s32[256,16]{0,1:T(8,128)} %param.12), kind=kLoop, calls=%fused_computation.120 | loop fusion | flops 12032 | bytes 17408 | tf_op jit(solution)/shard_map/reduce_sum | solution.py:45
  12.4 0.8 %copy.20 = s32[4,32,8]{2,1,0:T(8,128)S(1)} copy(s32[4,32,8]{1,2,0:T(8,128)} %param.14) | data formatting | bytes 8192 | tf_op args[6]
  13.2 0.7 %copy.19 = s32[4,32,8]{1,0,2:T(4,128)S(1)} copy(s32[4,32,8]{1,2,0:T(8,128)} %param.14) | data formatting | bytes 8192 | tf_op args[6]
  13.9 1.2 %fusion.142 = f32[256,512]{1,0:T(8,128)S(1)} fusion(bf16[256,512]{1,0:T(8,128)(2,1)} %param.8, bf16[512,512]{1,0:T(8,128)(2,1)S(1)} %copy-done), kind=kOutput, calls=%fused_computation.133 | convolution fusion | flops 134217728 | bytes 1310720 | tf_op jit(solution)/shard_map/dot_general | solution.py:49
  15.5 1.2 %fusion = bf16[256,512]{1,0:T(8,128)(2,1)S(1)} fusion(f32[256,512]{1,0:T(8,128)S(1)} %fusion.142, bf16[512,512]{1,0:T(8,128)(2,1)S(1)} %copy-done.5, bf16[64,512]{1,0:T(8,128)(2,1)S(1)} %collective-permute-done.1, bf16[64,512]{1,0:T(8,128)(2,1)S(1)} %collective-permute-done, bf16[256,512]{1,0:T(8,128)(2,1)S(1)} %copy-done.2, f32[256]{0:T(256)S(1)} %convert_reduce_fusion, ...), kind=kOutput, calls=%fused_computation.6 | convolution fusion | flops 242876416 | bytes 1721344 | tf_op jit(solution)/shard_map/dot_general | solution.py:50
  17.0 0.5 %convolution_convert_fusion = bf16[1024,512]{1,0:T(8,128)(2,1)S(1)} fusion(bf16[256,512]{1,0:T(8,128)(2,1)S(1)} %fusion, s32[1024]{0:T(1024)S(1)} %eq.447), kind=kOutput, calls=%fused_computation.1 | convolution fusion | flops 269221888 | bytes 1314816 | tf_op jit(solution)/shard_map/dot_general | solution.py:18
  17.5 0.9 %convolution_convert_fusion.3 = bf16[128,512]{1,0:T(8,128)(2,1)} fusion(bf16[256,512]{1,0:T(8,128)(2,1)S(1)} %fusion, s32[128]{0:T(128)S(1)} %eq.443), kind=kOutput, calls=%fused_computation.11 | convolution fusion | flops 33652736 | bytes 393728 | tf_op jit(solution)/shard_map/dot_general | solution.py:18
  18.4 3.3 %all-to-all-start = ((bf16[4,32,512]{2,1,0:T(8,128)(2,1)}), bf16[4,32,512]{2,1,0:T(8,128)(2,1)S(1)}, u32[]{:S(2)}, u32[]{:S(2)}) async-start(bf16[4,32,512]{2,1,0:T(8,128)(2,1)} %bitcast.18), calls=%async_computation | async-start | bytes 262144 | tf_op jit(solution)/shard_map/all_to_all | solution.py:57
  21.7 0.4 fusion.6
  22.1 4.2 %all-to-all-done = bf16[4,32,512]{2,1,0:T(8,128)(2,1)S(1)} async-done(((bf16[4,32,512]{2,1,0:T(8,128)(2,1)}), bf16[4,32,512]{2,1,0:T(8,128)(2,1)S(1)}, u32[]{:S(2)}, u32[]{:S(2)}) %all-to-all-start) | async-done | bytes 131104 | tf_op jit(solution)/shard_map/all_to_all | solution.py:57
  26.3 0.5 %fusion.35 = f32[4,32,1,8]{3,2,1,0:T(1,128)S(1)} fusion(bf16[4,32,8,512]{3,2,1,0:T(8,128)(2,1)S(1)} %bitcast.55, bf16[4,32,512,1]{2,1,0,3:T(8,128)(2,1)S(1)} %bitcast.57), kind=kOutput, calls=%fused_computation.62 | convolution fusion | flops 1048576 | bytes 1183744 | tf_op jit(solution)/shard_map/vad,vakd->vak/dot_general | solution.py:59
  27.0 1.4 %multiply_reduce_fusion = f32[4,32,512]{2,1,0:T(8,128)} fusion(f32[4,32,8]{2,1,0:T(8,128)S(1)} %copy.22, bf16[1024,512]{1,0:T(8,128)(2,1)S(1)} %convolution_convert_fusion), kind=kLoop, calls=%fused_computation | loop fusion | flops 1507328 | bytes 1314816 | tf_op jit(solution)/shard_map/reduce_sum | solution.py:76
  28.4 3.4 %all-to-all-start.1 = ((f32[4,32,512]{2,1,0:T(8,128)}), f32[4,32,512]{2,1,0:T(8,128)S(1)}, u32[]{:S(2)}, u32[]{:S(2)}) async-start(f32[4,32,512]{2,1,0:T(8,128)} %multiply_reduce_fusion), calls=%async_computation.1 | async-start | bytes 524288 | tf_op jit(solution)/shard_map/all_to_all | solution.py:77
  31.9 0.4 select_reduce_fusion
  32.3 5.5 %all-to-all-done.1 = f32[4,32,512]{2,1,0:T(8,128)S(1)} async-done(((f32[4,32,512]{2,1,0:T(8,128)}), f32[4,32,512]{2,1,0:T(8,128)S(1)}, u32[]{:S(2)}, u32[]{:S(2)}) %all-to-all-start.1) | async-done | bytes 262176 | tf_op jit(solution)/shard_map/all_to_all | solution.py:77
  37.8 0.6 %fusion.122 = f32[256,512]{1,0:T(8,128)S(1)} fusion(f32[128,512]{1,0:T(8,128)S(1)} %bitcast.56, s32[128]{0:T(128)S(1)} %eq.443), kind=kOutput, calls=%fused_computation.103 | convolution fusion | flops 201392128 | bytes 786944 | tf_op jit(solution)/shard_map/dot_general | solution.py:24
  38.4 0.4 convolution_add_fusion.1
  38.8 1.3 %fusion.1 = bf16[256,512]{1,0:T(8,128)(2,1)} fusion(f32[256,512]{1,0:T(8,128)S(1)} %convolution_add_fusion.1, bf16[256,512]{1,0:T(8,128)(2,1)S(1)} %get-tuple-element.23, bf16[256,512]{1,0:T(8,128)(2,1)S(1)} %convolution_convert_fusion.1, f32[512]{0:T(512)S(1)} %pad_maximum_fusion, s32[512]{0:T(512)S(1)} %pad_add_fusion), kind=kOutput, calls=%fused_computation.7 | convolution fusion | flops 806879232 | bytes 1314816 | tf_op jit(solution)/shard_map/dot_general | solution.py:24
  (27 shorter events, 0.9 us)
Async XLA Ops:
  0.6 13.3 %copy-start = (bf16[512,512]{1,0:T(8,128)(2,1)S(1)}, bf16[512,512]{1,0:T(8,128)(2,1)}, u32[]{:S(2)}) copy-start(bf16[512,512]{1,0:T(8,128)(2,1)} %param.9) | copy-start | bytes 1572868
  1.4 13.9 %copy-start.3 = (s32[4,32]{1,0:T(4,128)S(1)}, s32[4,32]{1,0:T(4,128)}, u32[]{:S(2)}) copy-start(s32[4,32]{1,0:T(4,128)} %param.13) | copy-start | bytes 1540
  1.4 14.0 %copy-start.4 = (s32[256,2]{0,1:T(2,128)S(1)}, s32[256,2]{0,1:T(2,128)}, u32[]{:S(2)}) copy-start(s32[256,2]{0,1:T(2,128)} %param.15) | copy-start | bytes 6148
  2.6 12.9 %copy-start.2 = (bf16[256,512]{1,0:T(8,128)(2,1)S(1)}, bf16[256,512]{1,0:T(8,128)(2,1)}, u32[]{:S(2)}) copy-start(bf16[256,512]{1,0:T(8,128)(2,1)} %param.8) | copy-start | bytes 786436
  2.6 12.9 %copy-start.5 = (bf16[512,512]{1,0:T(8,128)(2,1)S(1)}, bf16[512,512]{1,0:T(8,128)(2,1)}, u32[]{:S(2)}) copy-start(bf16[512,512]{1,0:T(8,128)(2,1)} %param.10) | copy-start | bytes 1572868
  2.6 12.9 %collective-permute-start = (bf16[64,512]{1,0:T(8,128)(2,1)S(1)}, bf16[64,512]{1,0:T(8,128)(2,1)S(1)}, u32[]{:S(2)}, u32[]{:S(2)}) collective-permute-start(bf16[64,512]{1,0:T(8,128)(2,1)S(1)} %convolution_convert_fusion.5), channel_id=1, source_target_pairs={{0,4},{4,8},{8,12},{12,16},{16,20},{20,24},{24,28},{1,5},{5,9},{9,... | collective-permute-start | bytes 196616 | tf_op jit(solution)/shard_map/ppermute | solution.py:12
  7.3 8.2 %collective-permute-start.1 = (bf16[64,512]{1,0:T(8,128)(2,1)S(1)}, bf16[64,512]{1,0:T(8,128)(2,1)S(1)}, u32[]{:S(2)}, u32[]{:S(2)}) collective-permute-start(bf16[64,512]{1,0:T(8,128)(2,1)S(1)} %convolution_convert_fusion.4), channel_id=1, source_target_pairs={{4,0},{8,4},{12,8},{16,12},{20,16},{24,20},{28,24},{5,1},{9,5},{13... | collective-permute-start | bytes 196616 | tf_op jit(solution)/shard_map/ppermute | solution.py:12
  16.7 5.0 %copy-start.1 = (bf16[256,512]{1,0:T(8,128)(2,1)}, bf16[256,512]{1,0:T(8,128)(2,1)S(1)}, u32[]{:S(2)}) copy-start(bf16[256,512]{1,0:T(8,128)(2,1)S(1)} %fusion) | copy-start | bytes 786436
  18.4 7.9 %all-to-all-start = ((bf16[4,32,512]{2,1,0:T(8,128)(2,1)}), bf16[4,32,512]{2,1,0:T(8,128)(2,1)S(1)}, u32[]{:S(2)}, u32[]{:S(2)}) async-start(bf16[4,32,512]{2,1,0:T(8,128)(2,1)} %bitcast.18), calls=%async_computation | async-start | bytes 262144 | tf_op jit(solution)/shard_map/all_to_all | solution.py:57
  28.4 9.4 %all-to-all-start.1 = ((f32[4,32,512]{2,1,0:T(8,128)}), f32[4,32,512]{2,1,0:T(8,128)S(1)}, u32[]{:S(2)}, u32[]{:S(2)}) async-start(f32[4,32,512]{2,1,0:T(8,128)} %multiply_reduce_fusion), calls=%async_computation.1 | async-start | bytes 524288 | tf_op jit(solution)/shard_map/all_to_all | solution.py:77
where the time goes:
time: 40.8 us; the launch traced here: 40.1 us
  starting transfers between devices  13.6 us (33%)
  waiting for transfers between devices  9.75 us (24%)
  matrix products  9.53 us (23%)
  local copies, waits for them, and re-layouts  3.84 us (9%)
  other arithmetic  2.55 us (6%)
  between operations  0.83 us (2%)
    ppermute x2, starting transfers between devices, passed_along(): return lax.ppermute(block, axis, route)  6.87 us
    all_to_all x1, waiting for transfers between devices, body(): lax.all_to_all(back, 'wide', split_axis=0, concat_axis=0, tiled=True)  5.53 us
    dot_general x6, matrix products, pick_rows(): jnp.dot(onehot, table, preferred_element_type=jnp.float32)  4.34 us
    all_to_all x1, waiting for transfers between devices, body(): lax.all_to_all(a_rows, 'wide', split_axis=0, concat_axis=0, tiled=True)  4.22 us
    all_to_all x1, starting transfers between devices, body(): lax.all_to_all(back, 'wide', split_axis=0, concat_axis=0, tiled=True)  3.41 us
    all_to_all x1, starting transfers between devices, body(): lax.all_to_all(a_rows, 'wide', split_axis=0, concat_axis=0, tiled=True)  3.33 us
    dot_general x2, matrix products, spread_rows(): jnp.dot(mixing, rows.astype(jnp.float32), precision=lax.Precision.HIGHEST...  1.86 us
    unnamed x14, local copies, waits for them, and re-layouts  1.56 us
  transfers between devices with their start and end apart: 4, of which 2 were waited for; matrix products, arithmetic and copies ran while one was open for 17% of the time, Pallas kernels for 0%

commit v1 on v0

v1 whole, which is shorter than its diff:
```python
import functools
import math

import jax
import jax.numpy as jnp
from jax import lax
from jax.experimental import pallas as pl
from jax.experimental.pallas import tpu as pltpu
from jax.sharding import PartitionSpec as P

MESH = pl.DeviceIdType.MESH
BF = jnp.bfloat16
F32 = jnp.float32


def dot(a, b):
    return jnp.dot(a, b, preferred_element_type=F32)


def dot_nt(a, b):
    return lax.dot_general(a, b, (((1,), (1,)), ((), ())), preferred_element_type=F32)


def dot_tn(a, b):
    return lax.dot_general(a, b, (((0,), (0,)), ((), ())), preferred_element_type=F32)


def marks(row, height):
    rows = lax.broadcasted_iota(jnp.int32, (height, row.shape[1]), 0)
    return jnp.where(rows == row, 1.0, 0.0)


def kernel(
    n_dom,
    n_wide,
    feat_in,
    ws_in,
    wn_in,
    bnd_in,
    nbr_in,
    anch_in,
    neg_in,
    pos_in,
    embed_out,
    grad_out,
    feat,
    ws,
    wn,
    bnd,
    nbr,
    anch,
    neg,
    pos,
    b_send,
    b_recv,
    a_send,
    a_recv,
    t_send,
    t_recv,
    embed_v,
    grad_v,
    own_sum,
    own_proj,
    load_sem,
    store_sem,
    bs_sem,
    br_sem,
    as_sem,
    ar_sem,
    ts_sem,
    tr_sem,
):
    node_dev, width = feat.shape
    slots = nbr.shape[0]
    bnd_rows = bnd.shape[2]
    peers, anch_n = anch.shape
    fan = neg.shape[1]
    scale = 1.0 / math.sqrt(width)
    d = lax.axis_index("dom")
    w = lax.axis_index("wide")
    has_prev = d > 0
    has_next = d < n_dom - 1

    loads = [
        pltpu.make_async_copy(src, dst, load_sem.at[i])
        for i, (src, dst) in enumerate(
            [
                (bnd_in, bnd),
                (feat_in, feat),
                (nbr_in, nbr),
                (anch_in, anch),
                (neg_in, neg),
                (pos_in, pos),
                (ws_in, ws),
                (wn_in, wn),
            ]
        )
    ]
    for load in loads:
        load.start()

    barrier = pltpu.get_barrier_semaphore()

    @pl.when(has_prev)
    def _():
        pl.semaphore_signal(barrier, inc=1, device_id=(d - 1, w), device_id_type=MESH)

    @pl.when(has_next)
    def _():
        pl.semaphore_signal(barrier, inc=1, device_id=(d + 1, w), device_id_type=MESH)

    partner = [lax.rem(w + o, n_wide) for o in range(n_wide)]
    for o in range(1, n_wide):
        pl.semaphore_signal(barrier, inc=1, device_id=(d, partner[o]), device_id_type=MESH)

    loads[0].wait()
    loads[1].wait()
    features = feat[...]
    b_send[0] = dot_tn(marks(bnd[0, 0:1, :], node_dev).astype(BF), features).astype(BF)
    b_send[1] = dot_tn(marks(bnd[0, 1:2, :], node_dev).astype(BF), features).astype(BF)

    arrivals = n_wide - 1 + has_prev.astype(jnp.int32) + has_next.astype(jnp.int32)
    pl.semaphore_wait(barrier, arrivals)

    up = pltpu.make_async_remote_copy(
        src_ref=b_send.at[0],
        dst_ref=b_recv.at[0],
        send_sem=bs_sem.at[0],
        recv_sem=br_sem.at[0],
        device_id=(d + 1, w),
        device_id_type=MESH,
    )
    down = pltpu.make_async_remote_copy(
        src_ref=b_send.at[1],
        dst_ref=b_recv.at[1],
        send_sem=bs_sem.at[1],
        recv_sem=br_sem.at[1],
        device_id=(d - 1, w),
        device_id_type=MESH,
    )

    @pl.when(has_next)
    def _():
        up.start()

    @pl.when(has_prev)
    def _():
        down.start()

    @pl.when(jnp.logical_not(has_prev))
    def _():
        b_recv[0] = jnp.zeros((bnd_rows, width), BF)

    @pl.when(jnp.logical_not(has_next))
    def _():
        b_recv[1] = jnp.zeros((bnd_rows, width), BF)

    loads[2].wait()
    table_rows = node_dev + 2 * bnd_rows
    counts_t = marks(nbr[0:1, :], table_rows)
    for slot in range(1, slots):
        counts_t = counts_t + marks(nbr[slot : slot + 1, :], table_rows)
    counts = counts_t.T
    inverse = 1.0 / jnp.sum(counts, axis=1, keepdims=True)
    counts = counts.astype(BF)
    own_sum[...] = dot(counts[:, :node_dev], features)
    counts_bnd = counts[:, node_dev:]

    loads[6].wait()
    own_proj[...] = dot(features, ws[...])

    loads[3].wait()
    a_row = jnp.concatenate([anch[v : v + 1, :] for v in range(peers)], axis=1)
    anchors_t = marks(a_row, node_dev)
    anchors_n = anchors_t.T.astype(BF)
    anchors_t = anchors_t.astype(BF)

    loads[4].wait()
    n_rows = jnp.concatenate([neg[v] for v in range(peers)], axis=1)
    mult_t = marks(n_rows[0:1, :], node_dev)
    for k in range(1, fan):
        mult_t = mult_t + marks(n_rows[k : k + 1, :], node_dev)
    mult = mult_t.T

    loads[5].wait()
    first = marks(pos[0:1, :], node_dev).astype(BF)
    second = marks(pos[1:2, :], node_dev).astype(BF)
    pairs = dot_nt(
        jnp.concatenate([first, second], axis=1), jnp.concatenate([second, first], axis=1)
    )
    loads[7].wait()

    @pl.when(has_prev)
    def _():
        up.wait_recv()

    @pl.when(has_next)
    def _():
        down.wait_recv()

    received = b_recv[...].reshape(2 * bnd_rows, width)
    mean = ((own_sum[...] + dot(counts_bnd, received)) * inverse).astype(BF)
    embed = (own_proj[...] + dot(mean, wn[...])).astype(BF)
    embed_v[...] = embed

    a_send[...] = dot(anchors_n, embed).astype(BF).reshape(peers, anch_n, width)

    def exchange(source, target, send, recv):
        return [
            pltpu.make_async_remote_copy(
                src_ref=source.at[partner[o]],
                dst_ref=target.at[w],
                send_sem=send.at[o - 1],
                recv_sem=recv.at[o - 1],
                device_id=(d, partner[o]),
                device_id_type=MESH,
            )
            for o in range(1, n_wide)
        ]

    out = exchange(a_send, a_recv, as_sem, ar_sem)
    for copy in out:
        copy.start()
    store_embed = pltpu.make_async_copy(embed_v, embed_out, store_sem.at[0])
    store_embed.start()
    a_recv[pl.ds(w, 1)] = a_send[pl.ds(w, 1)]

    c_pos = pairs * (jax.nn.sigmoid(dot_nt(embed, embed) * scale) - 1.0)
    own_sum[...] = dot(c_pos.astype(BF), embed)

    for copy in out:
        copy.wait_recv()
    got = a_recv[...].reshape(peers * anch_n, width)
    coef = (mult * jax.nn.sigmoid(dot_nt(got, embed) * scale)).astype(BF)
    t_send[...] = dot(coef, embed).astype(BF).reshape(peers, anch_n, width)
    back = exchange(t_send, t_recv, ts_sem, tr_sem)
    for copy in back:
        copy.start()
    t_recv[pl.ds(w, 1)] = t_send[pl.ds(w, 1)]
    own_sum[...] += dot_tn(coef, got)
    for copy in back:
        copy.wait_recv()
    terms = t_recv[...].reshape(peers * anch_n, width)
    grad_v[...] = (own_sum[...] + dot(anchors_t, terms)).astype(BF)
    store_grad = pltpu.make_async_copy(grad_v, grad_out, store_sem.at[1])
    store_grad.start()

    @pl.when(has_next)
    def _():
        up.wait_send()

    @pl.when(has_prev)
    def _():
        down.wait_send()

    for copy in out + back:
        copy.wait_send()
    store_embed.wait()
    store_grad.wait()


def body(n_dom, n_wide, features, w_self, w_neigh, boundary, neighbors, anchors, negatives, positives):
    node_dev, width = features.shape
    bnd_rows = boundary.shape[2]
    peers, anch_n = anchors.shape
    small = [boundary, neighbors.T, anchors, negatives.transpose(0, 2, 1), positives.T]
    block = (peers, anch_n, width)
    anywhere = pl.BlockSpec(memory_space=pl.ANY)
    return pl.pallas_call(
        functools.partial(kernel, n_dom, n_wide),
        out_shape=[jax.ShapeDtypeStruct((node_dev, width), BF)] * 2,
        in_specs=[anywhere] * 8,
        out_specs=[anywhere] * 2,
        scratch_shapes=[
            pltpu.VMEM(features.shape, BF),
            pltpu.VMEM(w_self.shape, BF),
            pltpu.VMEM(w_neigh.shape, BF),
        ]
        + [pltpu.VMEM(x.shape, jnp.int32) for x in small]
        + [pltpu.VMEM((2, bnd_rows, width), BF)] * 2
        + [pltpu.VMEM(block, BF)] * 4
        + [pltpu.VMEM((node_dev, width), BF)] * 2
        + [pltpu.VMEM((node_dev, width), F32)] * 2
        + [
            pltpu.SemaphoreType.DMA((8,)),
            pltpu.SemaphoreType.DMA((2,)),
            pltpu.SemaphoreType.DMA((2,)),
            pltpu.SemaphoreType.DMA((2,)),
        ]
        + [pltpu.SemaphoreType.DMA((n_wide - 1,))] * 4,
        compiler_params=pltpu.CompilerParams(
            collective_id=0, has_side_effects=True, vmem_limit_bytes=32 * 1024 * 1024
        ),
    )(features, w_self, w_neigh, *small)


def solution(mesh):
    return jax.shard_map(
        functools.partial(body, mesh.shape["dom"], mesh.shape["wide"]),
        mesh=mesh,
        in_specs=(
            P(("dom", "wide"), None),
            P(),
            P(),
            P(("dom", "wide"), None, None),
            P(("dom", "wide"), None),
            P(("dom", "wide"), None),
            P(("dom", "wide"), None, None),
            P(("dom", "wide"), None),
        ),
        out_specs=(P(("dom", "wide"), None), P(("dom", "wide"), None)),
        check_vma=False,
    )
```

time: 40.8 us -> 22.5 us (0.55)
  the two profiles are of different devices: /device:TPU:24 before, /device:TPU:9 now
where the time goes in v1:
time: 22.5 us; the launch traced here: 22.1 us
  Pallas kernels  14.9 us (66%)
  local copies, waits for them, and re-layouts  6.56 us (29%)
  between operations  0.67 us (3%)
    pallas_call x1, Pallas kernels, body(): pl.pallas_call(functools.partial(kernel, n_dom, n_wide), out_shape=[jax.S...  14.9 us
    unnamed x18, local copies, waits for them, and re-layouts  6.56 us

profile of v1, /device:TPU:9, one launch (start us, length us, event | category | flops | bytes accessed | tf_op | source)
XLA Modules:
  0.0 22.1 jit_solution(9499219690686421867)
XLA Ops:
  0.6 0.0 copy-start.6
  0.6 0.0 copy-start.5
  0.7 0.0 copy-start.7
  0.7 0.7 %copy-done.6 = s32[256,2]{0,1:T(2,128)S(1)} copy-done((s32[256,2]{0,1:T(2,128)S(1)}, s32[256,2]{0,1:T(2,128)}, u32[]{:S(2)}) %copy-start.6) | copy-done | bytes 2072
  1.3 0.0 copy-done.5
  1.3 0.0 copy-done.7
  1.3 0.0 copy-start
  1.3 1.0 %copy-done = bf16[512,512]{1,0:T(8,128)(2,1)S(1)} copy-done((bf16[512,512]{1,0:T(8,128)(2,1)S(1)}, bf16[512,512]{1,0:T(8,128)(2,1)}, u32[]{:S(2)}) %copy-start) | copy-done | bytes 524312
  2.4 0.0 copy-start.1
  2.4 1.0 %copy-done.1 = bf16[512,512]{1,0:T(8,128)(2,1)S(1)} copy-done((bf16[512,512]{1,0:T(8,128)(2,1)S(1)}, bf16[512,512]{1,0:T(8,128)(2,1)}, u32[]{:S(2)}) %copy-start.1) | copy-done | bytes 524312
  3.4 0.0 copy-start.2
  3.4 0.9 %copy-done.2 = bf16[256,512]{1,0:T(8,128)(2,1)S(1)} copy-done((bf16[256,512]{1,0:T(8,128)(2,1)S(1)}, bf16[256,512]{1,0:T(8,128)(2,1)}, u32[]{:S(2)}) %copy-start.2) | copy-done | bytes 262168
  4.4 0.0 copy-start.3
  4.4 0.7 %copy-done.3 = s32[256,16]{0,1:T(8,128)S(1)} copy-done((s32[256,16]{0,1:T(8,128)S(1)}, s32[256,16]{0,1:T(8,128)}, u32[]{:S(2)}) %copy-start.3) | copy-done | bytes 16408
  5.1 0.0 copy-start.4
  5.1 0.7 %copy-done.4 = s32[4,32,8]{1,2,0:T(8,128)S(1)} copy-done((s32[4,32,8]{1,2,0:T(8,128)S(1)}, s32[4,32,8]{1,2,0:T(8,128)}, u32[]{:S(2)}) %copy-start.4) | copy-done | bytes 4120
  5.8 14.9 %shard_map.95 = (bf16[256,512]{1,0:T(8,128)(2,1)S(1)}, bf16[256,512]{1,0:T(8,128)(2,1)S(1)}) custom-call(bf16[256,512]{1,0:T(8,128)(2,1)S(1)} %copy-done.2, bf16[512,512]{1,0:T(8,128)(2,1)S(1)} %copy-done, bf16[512,512]{1,0:T(8,128)(2,1)S(1)} %copy-done.1, s32[1,2,64]{2,1,0:T(2,128)S(1)} %copy-done.7, s32[16,256]{1,0:T(8,128)S(1)} %bitcast.3, ...), custom_call_target="tpu_custom_call" | custom-call | tf_op jit(solution)/shard_map/pallas_call | solution.py:269
  20.7 0.7 %copy.12 = bf16[256,512]{1,0:T(8,128)(2,1)} copy(bf16[256,512]{1,0:T(8,128)(2,1)S(1)} %get-tuple-element.4) | data formatting | bytes 524288
  21.4 0.7 %copy.13 = bf16[256,512]{1,0:T(8,128)(2,1)} copy(bf16[256,512]{1,0:T(8,128)(2,1)S(1)} %get-tuple-element.5) | data formatting | bytes 524288
Async XLA Ops:
  0.6 0.7 %copy-start.6 = (s32[256,2]{0,1:T(2,128)S(1)}, s32[256,2]{0,1:T(2,128)}, u32[]{:S(2)}) copy-start(s32[256,2]{0,1:T(2,128)} %param.15) | copy-start | bytes 6148
  0.6 0.7 %copy-start.5 = (s32[4,32]{1,0:T(4,128)S(1)}, s32[4,32]{1,0:T(4,128)}, u32[]{:S(2)}) copy-start(s32[4,32]{1,0:T(4,128)} %anch_in.1) | copy-start | bytes 1540
  0.7 0.7 %copy-start.7 = (s32[1,2,64]{2,1,0:T(2,128)S(1)}, s32[1,2,64]{2,1,0:T(2,128)}, u32[]{:S(2)}) copy-start(s32[1,2,64]{2,1,0:T(2,128)} %bnd_in.1) | copy-start | bytes 1540
  1.3 1.0 %copy-start = (bf16[512,512]{1,0:T(8,128)(2,1)S(1)}, bf16[512,512]{1,0:T(8,128)(2,1)}, u32[]{:S(2)}) copy-start(bf16[512,512]{1,0:T(8,128)(2,1)} %ws_in.1) | copy-start | bytes 1572868
  2.4 1.0 %copy-start.1 = (bf16[512,512]{1,0:T(8,128)(2,1)S(1)}, bf16[512,512]{1,0:T(8,128)(2,1)}, u32[]{:S(2)}) copy-start(bf16[512,512]{1,0:T(8,128)(2,1)} %wn_in.1) | copy-start | bytes 1572868
  3.4 0.9 %copy-start.2 = (bf16[256,512]{1,0:T(8,128)(2,1)S(1)}, bf16[256,512]{1,0:T(8,128)(2,1)}, u32[]{:S(2)}) copy-start(bf16[256,512]{1,0:T(8,128)(2,1)} %feat_in.1) | copy-start | bytes 786436
  4.4 0.7 %copy-start.3 = (s32[256,16]{0,1:T(8,128)S(1)}, s32[256,16]{0,1:T(8,128)}, u32[]{:S(2)}) copy-start(s32[256,16]{0,1:T(8,128)} %param.12) | copy-start | bytes 49156
  5.1 0.7 %copy-start.4 = (s32[4,32,8]{1,2,0:T(8,128)S(1)}, s32[4,32,8]{1,2,0:T(8,128)}, u32[]{:S(2)}) copy-start(s32[4,32,8]{1,2,0:T(8,128)} %param.14) | copy-start | bytes 12292

commit v2 on v1

--- a/solution.py
+++ b/solution.py
@@ -41,8 +41,8 @@
     anch_in,
     neg_in,
     pos_in,
-    embed_out,
-    grad_out,
+    embed_v,
+    grad_v,
     feat,
     ws,
     wn,
@@ -57,12 +57,9 @@
     a_recv,
     t_send,
     t_recv,
-    embed_v,
-    grad_v,
     own_sum,
     own_proj,
     load_sem,
-    store_sem,
     bs_sem,
     br_sem,
     as_sem,
@@ -175,19 +172,6 @@
     anchors_n = anchors_t.T.astype(BF)
     anchors_t = anchors_t.astype(BF)
 
-    loads[4].wait()
-    n_rows = jnp.concatenate([neg[v] for v in range(peers)], axis=1)
-    mult_t = marks(n_rows[0:1, :], node_dev)
-    for k in range(1, fan):
-        mult_t = mult_t + marks(n_rows[k : k + 1, :], node_dev)
-    mult = mult_t.T
-
-    loads[5].wait()
-    first = marks(pos[0:1, :], node_dev).astype(BF)
-    second = marks(pos[1:2, :], node_dev).astype(BF)
-    pairs = dot_nt(
-        jnp.concatenate([first, second], axis=1), jnp.concatenate([second, first], axis=1)
-    )
     loads[7].wait()
 
     @pl.when(has_prev)
@@ -221,12 +205,21 @@
     out = exchange(a_send, a_recv, as_sem, ar_sem)
     for copy in out:
         copy.start()
-    store_embed = pltpu.make_async_copy(embed_v, embed_out, store_sem.at[0])
-    store_embed.start()
     a_recv[pl.ds(w, 1)] = a_send[pl.ds(w, 1)]
 
-    c_pos = pairs * (jax.nn.sigmoid(dot_nt(embed, embed) * scale) - 1.0)
-    own_sum[...] = dot(c_pos.astype(BF), embed)
+    loads[4].wait()
+    n_rows = jnp.concatenate([neg[v] for v in range(peers)], axis=1)
+    mult_t = marks(n_rows[0:1, :], node_dev)
+    for k in range(1, fan):
+        mult_t = mult_t + marks(n_rows[k : k + 1, :], node_dev)
+    mult = mult_t.T
+
+    loads[5].wait()
+    first = marks(pos[0:1, :], node_dev).astype(BF)
+    second = marks(pos[1:2, :], node_dev).astype(BF)
+    pairs = dot_nt(
+        jnp.concatenate([first, second], axis=1), jnp.concatenate([second, first], axis=1)
+    )
 
     for copy in out:
         copy.wait_recv()
@@ -237,13 +230,13 @@
     for copy in back:
         copy.start()
     t_recv[pl.ds(w, 1)] = t_send[pl.ds(w, 1)]
+    c_pos = pairs * (jax.nn.sigmoid(dot_nt(embed, embed) * scale) - 1.0)
+    own_sum[...] = dot(c_pos.astype(BF), embed)
     own_sum[...] += dot_tn(coef, got)
     for copy in back:
         copy.wait_recv()
     terms = t_recv[...].reshape(peers * anch_n, width)
     grad_v[...] = (own_sum[...] + dot(anchors_t, terms)).astype(BF)
-    store_grad = pltpu.make_async_copy(grad_v, grad_out, store_sem.at[1])
-    store_grad.start()
 
     @pl.when(has_next)
     def _():
@@ -255,8 +248,17 @@
 
     for copy in out + back:
         copy.wait_send()
-    store_embed.wait()
-    store_grad.wait()
+
+
+def store_kernel(embed_v, grad_v, embed_out, grad_out, sem):
+    stores = [
+        pltpu.make_async_copy(embed_v, embed_out, sem.at[0]),
+        pltpu.make_async_copy(grad_v, grad_out, sem.at[1]),
+    ]
+    for store in stores:
+        store.start()
+    for store in stores:
+        store.wait()
 
 
 def body(n_dom, n_wide, features, w_self, w_neigh, boundary, neighbors, anchors, negatives, positives):
@@ -265,12 +267,14 @@
     peers, anch_n = anchors.shape
     small = [boundary, neighbors.T, anchors, negatives.transpose(0, 2, 1), positives.T]
     block = (peers, anch_n, width)
-    anywhere = pl.BlockSpec(memory_space=pl.ANY)
-    return pl.pallas_call(
+    far = pl.BlockSpec(memory_space=pltpu.HBM)
+    near = pl.BlockSpec(memory_space=pltpu.VMEM)
+    results = [jax.ShapeDtypeStruct((node_dev, width), BF)] * 2
+    held = pl.pallas_call(
         functools.partial(kernel, n_dom, n_wide),
-        out_shape=[jax.ShapeDtypeStruct((node_dev, width), BF)] * 2,
-        in_specs=[anywhere] * 8,
-        out_specs=[anywhere] * 2,
+        out_shape=[pltpu.VMEM((node_dev, width), BF)] * 2,
+        in_specs=[far] * 8,
+        out_specs=[near] * 2,
         scratch_shapes=[
             pltpu.VMEM(features.shape, BF),
             pltpu.VMEM(w_self.shape, BF),
@@ -279,11 +283,9 @@
         + [pltpu.VMEM(x.shape, jnp.int32) for x in small]
         + [pltpu.VMEM((2, bnd_rows, width), BF)] * 2
         + [pltpu.VMEM(block, BF)] * 4
-        + [pltpu.VMEM((node_dev, width), BF)] * 2
         + [pltpu.VMEM((node_dev, width), F32)] * 2
         + [
             pltpu.SemaphoreType.DMA((8,)),
-            pltpu.SemaphoreType.DMA((2,)),
             pltpu.SemaphoreType.DMA((2,)),
             pltpu.SemaphoreType.DMA((2,)),
         ]
@@ -291,7 +293,14 @@
         compiler_params=pltpu.CompilerParams(
             collective_id=0, has_side_effects=True, vmem_limit_bytes=32 * 1024 * 1024
         ),
-    )(features, w_self, w_neigh, *small)
+    )(*[pltpu.with_memory_space_constraint(x, pltpu.HBM) for x in (features, w_self, w_neigh, *small)])
+    return pl.pallas_call(
+        store_kernel,
+        out_shape=results,
+        in_specs=[near] * 2,
+        out_specs=[far] * 2,
+        scratch_shapes=[pltpu.SemaphoreType.DMA((2,))],
+    )(*held)
 
 
 def solution(mesh):

time: 22.5 us -> 18.9 us (0.84); the launches traced: 22.1 us -> 18.8 us
  local copies, waits for them, and re-layouts: 6.56 us -> 1.39 us
  Pallas kernels: 14.9 us -> 16.8 us
    unnamed x18 -> x4, local copies, waits for them, and re-layouts: 6.56 us -> 1.39 us
    pallas_call x1 -> x2, Pallas kernels: 14.9 us -> 16.8 us  [the longest x1 14.9 us: body(): pl.pallas_call(functools.partial(kernel, n_dom, n_wide), out_shape=[pltpu...]
where the time goes in v2:
time: 18.9 us; the launch traced here: 18.8 us
  Pallas kernels  16.8 us (89%)
  local copies, waits for them, and re-layouts  1.39 us (7%)
  between operations  0.65 us (3%)
    pallas_call x1, Pallas kernels, body(): pl.pallas_call(functools.partial(kernel, n_dom, n_wide), out_shape=[pltpu...  14.9 us
    pallas_call x1, Pallas kernels, body(): pl.pallas_call(store_kernel, out_shape=results, in_specs=[near] * 2, out_...  1.83 us
    unnamed x4, local copies, waits for them, and re-layouts  1.39 us

profile of v2, /device:TPU:9, one launch (start us, length us, event | category | flops | bytes accessed | tf_op | source)
XLA Modules:
  0.0 18.8 jit_solution(10741494817849695870)
XLA Ops:
  0.6 14.9 %shard_map.95 = (bf16[256,512]{1,0:T(8,128)(2,1)S(1)}, bf16[256,512]{1,0:T(8,128)(2,1)S(1)}) custom-call(bf16[256,512]{1,0:T(8,128)(2,1)} %feat_in.1, bf16[512,512]{1,0:T(8,128)(2,1)} %ws_in.1, bf16[512,512]{1,0:T(8,128)(2,1)} %wn_in.1, s32[1,2,64]{2,1,0:T(2,128)} %bnd_in.1, s32[16,256]{1,0:T(8,128)} %bitcast.3, s32[4,32]{1,0:T(4,128)} %anch_in.1, ...), custom_call_target="tpu_custom_call" | custom-call | tf_op jit(solution)/shard_map/pallas_call | solution.py:273
  15.6 0.0 copy-start
  15.6 0.7 %copy-done = bf16[256,512]{1,0:T(8,128)(2,1)} copy-done((bf16[256,512]{1,0:T(8,128)(2,1)}, bf16[256,512]{1,0:T(8,128)(2,1)S(1)}, u32[]{:S(2)}) %copy-start) | copy-done | bytes 262168
  16.2 0.0 copy-start.1
  16.3 0.7 %copy-done.1 = bf16[256,512]{1,0:T(8,128)(2,1)} copy-done((bf16[256,512]{1,0:T(8,128)(2,1)}, bf16[256,512]{1,0:T(8,128)(2,1)S(1)}, u32[]{:S(2)}) %copy-start.1) | copy-done | bytes 262168
  17.0 1.8 %shard_map.96 = (bf16[256,512]{1,0:T(8,128)(2,1)}, bf16[256,512]{1,0:T(8,128)(2,1)}) custom-call(bf16[256,512]{1,0:T(8,128)(2,1)} %copy-done, bf16[256,512]{1,0:T(8,128)(2,1)} %copy-done.1), custom_call_target="tpu_custom_call" | custom-call | tf_op jit(solution)/shard_map/pallas_call | solution.py:297
Async XLA Ops:
  15.6 0.7 %copy-start = (bf16[256,512]{1,0:T(8,128)(2,1)}, bf16[256,512]{1,0:T(8,128)(2,1)S(1)}, u32[]{:S(2)}) copy-start(bf16[256,512]{1,0:T(8,128)(2,1)S(1)} %get-tuple-element.4.embed_v) | copy-start | bytes 786436
  16.2 0.7 %copy-start.1 = (bf16[256,512]{1,0:T(8,128)(2,1)}, bf16[256,512]{1,0:T(8,128)(2,1)S(1)}, u32[]{:S(2)}) copy-start(bf16[256,512]{1,0:T(8,128)(2,1)S(1)} %get-tuple-element.5.grad_v) | copy-start | bytes 786436

commit v3 on v2

--- a/solution.py
+++ b/solution.py
@@ -28,6 +28,17 @@
 def marks(row, height):
     rows = lax.broadcasted_iota(jnp.int32, (height, row.shape[1]), 0)
     return jnp.where(rows == row, 1.0, 0.0)
+
+
+def peer_at(w, o, n):
+    if n & (n - 1):
+        return lax.rem(w + o + n, n)
+    bit = 1
+    while bit <= o:
+        if o & bit:
+            w = w + bit * (1 - 2 * lax.rem(w // bit, 2))
+        bit *= 2
+    return w
 
 
 def kernel(
@@ -57,6 +68,8 @@
     a_recv,
     t_send,
     t_recv,
+    mult,
+    coef,
     own_sum,
     own_proj,
     load_sem,
@@ -106,15 +119,17 @@
     def _():
         pl.semaphore_signal(barrier, inc=1, device_id=(d + 1, w), device_id_type=MESH)
 
-    partner = [lax.rem(w + o, n_wide) for o in range(n_wide)]
+    partner = [peer_at(w, o, n_wide) for o in range(n_wide)]
+    origin = partner if n_wide & (n_wide - 1) == 0 else [peer_at(w, -o, n_wide) for o in range(n_wide)]
     for o in range(1, n_wide):
         pl.semaphore_signal(barrier, inc=1, device_id=(d, partner[o]), device_id_type=MESH)
 
     loads[0].wait()
     loads[1].wait()
     features = feat[...]
-    b_send[0] = dot_tn(marks(bnd[0, 0:1, :], node_dev).astype(BF), features).astype(BF)
-    b_send[1] = dot_tn(marks(bnd[0, 1:2, :], node_dev).astype(BF), features).astype(BF)
+    b_row = jnp.concatenate([bnd[0, 0:1, :], bnd[0, 1:2, :]], axis=1)
+    picked = dot_tn(marks(b_row, node_dev).astype(BF), features)
+    b_send[...] = picked.astype(BF).reshape(2, bnd_rows, width)
 
     arrivals = n_wide - 1 + has_prev.astype(jnp.int32) + has_next.astype(jnp.int32)
     pl.semaphore_wait(barrier, arrivals)
@@ -157,62 +172,70 @@
     counts_t = marks(nbr[0:1, :], table_rows)
     for slot in range(1, slots):
         counts_t = counts_t + marks(nbr[slot : slot + 1, :], table_rows)
-    counts = counts_t.T
-    inverse = 1.0 / jnp.sum(counts, axis=1, keepdims=True)
-    counts = counts.astype(BF)
-    own_sum[...] = dot(counts[:, :node_dev], features)
-    counts_bnd = counts[:, node_dev:]
-
-    loads[6].wait()
-    own_proj[...] = dot(features, ws[...])
+    counts = counts_t.T.astype(BF)
 
     loads[3].wait()
     a_row = jnp.concatenate([anch[v : v + 1, :] for v in range(peers)], axis=1)
     anchors_t = marks(a_row, node_dev)
     anchors_n = anchors_t.T.astype(BF)
     anchors_t = anchors_t.astype(BF)
-
-    loads[7].wait()
-
-    @pl.when(has_prev)
-    def _():
-        up.wait_recv()
-
-    @pl.when(has_next)
-    def _():
-        down.wait_recv()
-
-    received = b_recv[...].reshape(2 * bnd_rows, width)
-    mean = ((own_sum[...] + dot(counts_bnd, received)) * inverse).astype(BF)
-    embed = (own_proj[...] + dot(mean, wn[...])).astype(BF)
-    embed_v[...] = embed
-
-    a_send[...] = dot(anchors_n, embed).astype(BF).reshape(peers, anch_n, width)
-
-    def exchange(source, target, send, recv):
-        return [
-            pltpu.make_async_remote_copy(
-                src_ref=source.at[partner[o]],
-                dst_ref=target.at[w],
-                send_sem=send.at[o - 1],
-                recv_sem=recv.at[o - 1],
-                device_id=(d, partner[o]),
-                device_id_type=MESH,
-            )
-            for o in range(1, n_wide)
-        ]
-
-    out = exchange(a_send, a_recv, as_sem, ar_sem)
-    for copy in out:
-        copy.start()
-    a_recv[pl.ds(w, 1)] = a_send[pl.ds(w, 1)]
+    n_anch = peers * anch_n
+    picked_counts = dot(anchors_n, counts)
+    counts_a = picked_counts.astype(BF)
+    inverse_a = 1.0 / jnp.sum(picked_counts, axis=1, keepdims=True)
+    inverse = 1.0 / jnp.sum(counts.astype(F32), axis=1, keepdims=True)
+    both = jnp.concatenate([counts_a[:, :node_dev], counts[:, :node_dev]], axis=0)
+    own_sum[...] = dot(both, features)
+
+    loads[6].wait()
+    feat_a = dot(anchors_n, features).astype(BF)
+    own_proj[...] = dot(jnp.concatenate([feat_a, features], axis=0), ws[...])
 
     loads[4].wait()
     n_rows = jnp.concatenate([neg[v] for v in range(peers)], axis=1)
     mult_t = marks(n_rows[0:1, :], node_dev)
     for k in range(1, fan):
         mult_t = mult_t + marks(n_rows[k : k + 1, :], node_dev)
-    mult = mult_t.T
+    mult[...] = mult_t.T.reshape(peers, anch_n, node_dev)
+    loads[7].wait()
+
+    @pl.when(has_prev)
+    def _():
+        up.wait_recv()
+
+    @pl.when(has_next)
+    def _():
+        down.wait_recv()
+
+    received = b_recv[...].reshape(2 * bnd_rows, width)
+
+    def embedding(rows, bnd_counts, inv):
+        mean = ((own_sum[rows, :] + dot(bnd_counts, received)) * inv).astype(BF)
+        return (own_proj[rows, :] + dot(mean, wn[...])).astype(BF)
+
+    anchor_embed = embedding(pl.ds(0, n_anch), counts_a[:, node_dev:], inverse_a)
+    a_send[...] = anchor_embed.reshape(peers, anch_n, width)
+
+    def exchange(source, target, send, recv, to):
+        return [
+            pltpu.make_async_remote_copy(
+                src_ref=source.at[to[o]],
+                dst_ref=target.at[w],
+                send_sem=send.at[o - 1],
+                recv_sem=recv.at[o - 1],
+                device_id=(d, to[o]),
+                device_id_type=MESH,
+            )
+            for o in range(1, n_wide)
+        ]
+
+    out = exchange(a_send, a_recv, as_sem, ar_sem, partner)
+    for copy in out[1:] + out[:1]:
+        copy.start()
+    a_recv[pl.ds(w, 1)] = a_send[pl.ds(w, 1)]
+
+    embed = embedding(pl.ds(n_anch, node_dev), counts[:, node_dev:], inverse)
+    embed_v[...] = embed
 
     loads[5].wait()
     first = marks(pos[0:1, :], node_dev).astype(BF)
@@ -221,22 +244,27 @@
         jnp.concatenate([first, second], axis=1), jnp.concatenate([second, first], axis=1)
     )
 
-    for copy in out:
+    back = exchange(t_send, t_recv, ts_sem, tr_sem, origin)
+
+    def answer(v):
+        score = dot_nt(a_recv[v], embed) * scale
+        c = (mult[v] * jax.nn.sigmoid(score)).astype(BF)
+        coef[v] = c
+        return dot(c, embed).astype(BF)
+
+    t_recv[w] = answer(w)
+    for copy, reply, v in zip(out, back, origin[1:]):
         copy.wait_recv()
-    got = a_recv[...].reshape(peers * anch_n, width)
-    coef = (mult * jax.nn.sigmoid(dot_nt(got, embed) * scale)).astype(BF)
-    t_send[...] = dot(coef, embed).astype(BF).reshape(peers, anch_n, width)
-    back = exchange(t_send, t_recv, ts_sem, tr_sem)
-    for copy in back:
-        copy.start()
-    t_recv[pl.ds(w, 1)] = t_send[pl.ds(w, 1)]
+        t_send[v] = answer(v)
+        reply.start()
+
     c_pos = pairs * (jax.nn.sigmoid(dot_nt(embed, embed) * scale) - 1.0)
-    own_sum[...] = dot(c_pos.astype(BF), embed)
-    own_sum[...] += dot_tn(coef, got)
+    got = a_recv[...].reshape(n_anch, width)
+    grad = dot(c_pos.astype(BF), embed) + dot_tn(coef[...].reshape(n_anch, node_dev), got)
     for copy in back:
         copy.wait_recv()
-    terms = t_recv[...].reshape(peers * anch_n, width)
-    grad_v[...] = (own_sum[...] + dot(anchors_t, terms)).astype(BF)
+    terms = t_recv[...].reshape(n_anch, width)
+    grad_v[...] = (grad + dot(anchors_t, terms)).astype(BF)
 
     @pl.when(has_next)
     def _():
@@ -283,7 +311,11 @@
         + [pltpu.VMEM(x.shape, jnp.int32) for x in small]
         + [pltpu.VMEM((2, bnd_rows, width), BF)] * 2
         + [pltpu.VMEM(block, BF)] * 4
-        + [pltpu.VMEM((node_dev, width), F32)] * 2
+        + [
+            pltpu.VMEM((peers, anch_n, node_dev), F32),
+            pltpu.VMEM((peers, anch_n, node_dev), BF),
+        ]
+        + [pltpu.VMEM((peers * anch_n + node_dev, width), F32)] * 2
         + [
             pltpu.SemaphoreType.DMA((8,)),
             pltpu.SemaphoreType.DMA((2,)),
@@ -300,7 +332,8 @@
         in_specs=[near] * 2,
         out_specs=[far] * 2,
         scratch_shapes=[pltpu.SemaphoreType.DMA((2,))],
-    )(*held)
+        compiler_params=pltpu.CompilerParams(vmem_limit_bytes=4 * 1024 * 1024),
+    )(*[pltpu.with_memory_space_constraint(x, pltpu.VMEM) for x in held])
 
 
 def solution(mesh):

time: 18.9 us -> 15.9 us (0.84)
  Pallas kernels: 16.8 us -> 15.1 us
  local copies, waits for them, and re-layouts: 1.39 us -> 0 us
    unnamed x4 -> x0, local copies, waits for them, and re-layouts: 1.39 us -> none
    pallas_call x1, Pallas kernels: 1.83 us -> 0.81 us  [body(): pl.pallas_call(store_kernel, out_shape=results, in_specs=[near] * 2, out_...]
    pallas_call x1, Pallas kernels: 14.9 us -> 14.3 us  [body(): pl.pallas_call(functools.partial(kernel, n_dom, n_wide), out_shape=[pltpu...]
where the time goes in v3:
time: 15.9 us; the launch traced here: 15.8 us
  Pallas kernels  15.1 us (95%)
  between operations  0.64 us (4%)
    pallas_call x1, Pallas kernels, body(): pl.pallas_call(functools.partial(kernel, n_dom, n_wide), out_shape=[pltpu...  14.3 us
    pallas_call x1, Pallas kernels, body(): pl.pallas_call(store_kernel, out_shape=results, in_specs=[near] * 2, out_...  0.81 us

profile of v3, /device:TPU:9, one launch (start us, length us, event | category | flops | bytes accessed | tf_op | source)
XLA Modules:
  0.0 15.8 jit_solution(17035250008120081263)
XLA Ops:
  0.6 14.3 %shard_map.95 = (bf16[256,512]{1,0:T(8,128)(2,1)S(1)}, bf16[256,512]{1,0:T(8,128)(2,1)S(1)}) custom-call(bf16[256,512]{1,0:T(8,128)(2,1)} %feat_in.1, bf16[512,512]{1,0:T(8,128)(2,1)} %ws_in.1, bf16[512,512]{1,0:T(8,128)(2,1)} %wn_in.1, s32[1,2,64]{2,1,0:T(2,128)} %bnd_in.1, s32[16,256]{1,0:T(8,128)} %bitcast.3, s32[4,32]{1,0:T(4,128)} %anch_in.1, ...), custom_call_target="tpu_custom_call" | custom-call | tf_op jit(solution)/shard_map/pallas_call | solution.py:301
  15.0 0.8 %shard_map.96 = (bf16[256,512]{1,0:T(8,128)(2,1)}, bf16[256,512]{1,0:T(8,128)(2,1)}) custom-call(bf16[256,512]{1,0:T(8,128)(2,1)S(1)} %get-tuple-element.4.embed_v, bf16[256,512]{1,0:T(8,128)(2,1)S(1)} %get-tuple-element.5.grad_v), custom_call_target="tpu_custom_call" | custom-call | tf_op jit(solution)/shard_map/pallas_call | solution.py:329

commit v4 on v3

--- a/solution.py
+++ b/solution.py
@@ -106,7 +106,7 @@
             ]
         )
     ]
-    for load in loads:
+    for load in loads[:2]:
         load.start()
 
     barrier = pltpu.get_barrier_semaphore()
@@ -125,10 +125,13 @@
         pl.semaphore_signal(barrier, inc=1, device_id=(d, partner[o]), device_id_type=MESH)
 
     loads[0].wait()
+    b_row = jnp.concatenate([bnd[0, 0:1, :], bnd[0, 1:2, :]], axis=1)
+    b_pick = marks(b_row, node_dev).T.astype(BF)
     loads[1].wait()
+    for load in loads[2:]:
+        load.start()
     features = feat[...]
-    b_row = jnp.concatenate([bnd[0, 0:1, :], bnd[0, 1:2, :]], axis=1)
-    picked = dot_tn(marks(b_row, node_dev).astype(BF), features)
+    picked = dot(b_pick, features)
     b_send[...] = picked.astype(BF).reshape(2, bnd_rows, width)
 
     arrivals = n_wide - 1 + has_prev.astype(jnp.int32) + has_next.astype(jnp.int32)
@@ -237,27 +240,26 @@
     embed = embedding(pl.ds(n_anch, node_dev), counts[:, node_dev:], inverse)
     embed_v[...] = embed
 
+    back = exchange(t_send, t_recv, ts_sem, tr_sem, origin)
+
+    def answer(v):
+        score = dot_nt(a_recv[v], embed) * scale
+        c = (mult[v] * jax.nn.sigmoid(score)).astype(BF)
+        coef[v] = c
+        return dot(c, embed).astype(BF)
+
+    for copy, reply, v in zip(out, back, origin[1:]):
+        copy.wait_recv()
+        t_send[v] = answer(v)
+        reply.start()
+
     loads[5].wait()
     first = marks(pos[0:1, :], node_dev).astype(BF)
     second = marks(pos[1:2, :], node_dev).astype(BF)
     pairs = dot_nt(
         jnp.concatenate([first, second], axis=1), jnp.concatenate([second, first], axis=1)
     )
-
-    back = exchange(t_send, t_recv, ts_sem, tr_sem, origin)
-
-    def answer(v):
-        score = dot_nt(a_recv[v], embed) * scale
-        c = (mult[v] * jax.nn.sigmoid(score)).astype(BF)
-        coef[v] = c
-        return dot(c, embed).astype(BF)
-
     t_recv[w] = answer(w)
-    for copy, reply, v in zip(out, back, origin[1:]):
-        copy.wait_recv()
-        t_send[v] = answer(v)
-        reply.start()
-
     c_pos = pairs * (jax.nn.sigmoid(dot_nt(embed, embed) * scale) - 1.0)
     got = a_recv[...].reshape(n_anch, width)
     grad = dot(c_pos.astype(BF), embed) + dot_tn(coef[...].reshape(n_anch, node_dev), got)

time: 15.9 us -> 15.9 us (level)
  no operation moved by 1% of the time
where the time goes in v4:
time: 15.9 us; the launch traced here: 15.8 us
  Pallas kernels  15.1 us (95%)
  between operations  0.64 us (4%)
    pallas_call x1, Pallas kernels, body(): pl.pallas_call(functools.partial(kernel, n_dom, n_wide), out_shape=[pltpu...  14.3 us
    pallas_call x1, Pallas kernels, body(): pl.pallas_call(store_kernel, out_shape=results, in_specs=[near] * 2, out_...  0.81 us

profile of v4, /device:TPU:9, one launch (start us, length us, event | category | flops | bytes accessed | tf_op | source)
XLA Modules:
  0.0 15.8 jit_solution(13691442068562792818)
XLA Ops:
  0.6 14.3 %shard_map.95 = (bf16[256,512]{1,0:T(8,128)(2,1)S(1)}, bf16[256,512]{1,0:T(8,128)(2,1)S(1)}) custom-call(bf16[256,512]{1,0:T(8,128)(2,1)} %feat_in.1, bf16[512,512]{1,0:T(8,128)(2,1)} %ws_in.1, bf16[512,512]{1,0:T(8,128)(2,1)} %wn_in.1, s32[1,2,64]{2,1,0:T(2,128)} %bnd_in.1, s32[16,256]{1,0:T(8,128)} %bitcast.3, s32[4,32]{1,0:T(4,128)} %anch_in.1, ...), custom_call_target="tpu_custom_call" | custom-call | tf_op jit(solution)/shard_map/pallas_call | solution.py:303
  14.9 0.8 %shard_map.96 = (bf16[256,512]{1,0:T(8,128)(2,1)}, bf16[256,512]{1,0:T(8,128)(2,1)}) custom-call(bf16[256,512]{1,0:T(8,128)(2,1)S(1)} %get-tuple-element.4.embed_v, bf16[256,512]{1,0:T(8,128)(2,1)S(1)} %get-tuple-element.5.grad_v), custom_call_target="tpu_custom_call" | custom-call | tf_op jit(solution)/shard_map/pallas_call | solution.py:331

commit v5 on v4

--- a/solution.py
+++ b/solution.py
@@ -70,6 +70,7 @@
     t_recv,
     mult,
     coef,
+    embed_t,
     own_sum,
     own_proj,
     load_sem,
@@ -154,11 +155,17 @@
         device_id_type=MESH,
     )
 
+    even = lax.rem(d, 2) == 0
+
+    @pl.when(jnp.logical_and(has_prev, even))
+    def _():
+        down.start()
+
     @pl.when(has_next)
     def _():
         up.start()
 
-    @pl.when(has_prev)
+    @pl.when(jnp.logical_and(has_prev, jnp.logical_not(even)))
     def _():
         down.start()
 
@@ -233,17 +240,18 @@
         ]
 
     out = exchange(a_send, a_recv, as_sem, ar_sem, partner)
-    for copy in out[1:] + out[:1]:
+    for copy in out:
         copy.start()
     a_recv[pl.ds(w, 1)] = a_send[pl.ds(w, 1)]
 
     embed = embedding(pl.ds(n_anch, node_dev), counts[:, node_dev:], inverse)
     embed_v[...] = embed
+    embed_t[...] = embed.T
 
     back = exchange(t_send, t_recv, ts_sem, tr_sem, origin)
 
     def answer(v):
-        score = dot_nt(a_recv[v], embed) * scale
+        score = dot(a_recv[v], embed_t[...]) * scale
         c = (mult[v] * jax.nn.sigmoid(score)).astype(BF)
         coef[v] = c
         return dot(c, embed).astype(BF)
@@ -260,7 +268,7 @@
         jnp.concatenate([first, second], axis=1), jnp.concatenate([second, first], axis=1)
     )
     t_recv[w] = answer(w)
-    c_pos = pairs * (jax.nn.sigmoid(dot_nt(embed, embed) * scale) - 1.0)
+    c_pos = pairs * (jax.nn.sigmoid(dot(embed, embed_t[...]) * scale) - 1.0)
     got = a_recv[...].reshape(n_anch, width)
     grad = dot(c_pos.astype(BF), embed) + dot_tn(coef[...].reshape(n_anch, node_dev), got)
     for copy in back:
@@ -316,6 +324,7 @@
         + [
             pltpu.VMEM((peers, anch_n, node_dev), F32),
             pltpu.VMEM((peers, anch_n, node_dev), BF),
+            pltpu.VMEM((width, node_dev), BF),
         ]
         + [pltpu.VMEM((peers * anch_n + node_dev, width), F32)] * 2
         + [

time: 15.9 us -> 15.8 us (level)
  no operation moved by 1% of the time
where the time goes in v5:
time: 15.8 us; the launch traced here: 15.6 us
  Pallas kernels  15 us (95%)
  between operations  0.64 us (4%)
    pallas_call x1, Pallas kernels, body(): pl.pallas_call(functools.partial(kernel, n_dom, n_wide), out_shape=[pltpu...  14.2 us
    pallas_call x1, Pallas kernels, body(): pl.pallas_call(store_kernel, out_shape=results, in_specs=[near] * 2, out_...  0.81 us

profile of v5, /device:TPU:9, one launch (start us, length us, event | category | flops | bytes accessed | tf_op | source)
XLA Modules:
  0.0 15.6 jit_solution(8888137324782890910)
XLA Ops:
  0.6 14.2 %shard_map.95 = (bf16[256,512]{1,0:T(8,128)(2,1)S(1)}, bf16[256,512]{1,0:T(8,128)(2,1)S(1)}) custom-call(bf16[256,512]{1,0:T(8,128)(2,1)} %feat_in.1, bf16[512,512]{1,0:T(8,128)(2,1)} %ws_in.1, bf16[512,512]{1,0:T(8,128)(2,1)} %wn_in.1, s32[1,2,64]{2,1,0:T(2,128)} %bnd_in.1, s32[16,256]{1,0:T(8,128)} %bitcast.3, s32[4,32]{1,0:T(4,128)} %anch_in.1, ...), custom_call_target="tpu_custom_call" | custom-call | tf_op jit(solution)/shard_map/pallas_call | solution.py:311
  14.8 0.8 %shard_map.96 = (bf16[256,512]{1,0:T(8,128)(2,1)}, bf16[256,512]{1,0:T(8,128)(2,1)}) custom-call(bf16[256,512]{1,0:T(8,128)(2,1)S(1)} %get-tuple-element.4.embed_v, bf16[256,512]{1,0:T(8,128)(2,1)S(1)} %get-tuple-element.5.grad_v), custom_call_target="tpu_custom_call" | custom-call | tf_op jit(solution)/shard_map/pallas_call | solution.py:340

commit v6 on v5

--- a/solution.py
+++ b/solution.py
@@ -107,8 +107,6 @@
             ]
         )
     ]
-    for load in loads[:2]:
-        load.start()
 
     barrier = pltpu.get_barrier_semaphore()
 
@@ -124,6 +122,9 @@
     origin = partner if n_wide & (n_wide - 1) == 0 else [peer_at(w, -o, n_wide) for o in range(n_wide)]
     for o in range(1, n_wide):
         pl.semaphore_signal(barrier, inc=1, device_id=(d, partner[o]), device_id_type=MESH)
+
+    for load in loads[:2]:
+        load.start()
 
     loads[0].wait()
     b_row = jnp.concatenate([bnd[0, 0:1, :], bnd[0, 1:2, :]], axis=1)
@@ -133,49 +134,53 @@
         load.start()
     features = feat[...]
     picked = dot(b_pick, features)
-    b_send[...] = picked.astype(BF).reshape(2, bnd_rows, width)
+    halves = b_send.shape[0]
+    half = width // halves
+    for h in range(halves):
+        b_send[h] = picked[:, h * half : (h + 1) * half].astype(BF).reshape(2, bnd_rows, half)
 
     arrivals = n_wide - 1 + has_prev.astype(jnp.int32) + has_next.astype(jnp.int32)
     pl.semaphore_wait(barrier, arrivals)
 
-    up = pltpu.make_async_remote_copy(
-        src_ref=b_send.at[0],
-        dst_ref=b_recv.at[0],
-        send_sem=bs_sem.at[0],
-        recv_sem=br_sem.at[0],
-        device_id=(d + 1, w),
-        device_id_type=MESH,
-    )
-    down = pltpu.make_async_remote_copy(
-        src_ref=b_send.at[1],
-        dst_ref=b_recv.at[1],
-        send_sem=bs_sem.at[1],
-        recv_sem=br_sem.at[1],
-        device_id=(d - 1, w),
-        device_id_type=MESH,
-    )
-
+    def boundary_copies(side, step):
+        return [
+            pltpu.make_async_remote_copy(
+                src_ref=b_send.at[h, side],
+                dst_ref=b_recv.at[h, side],
+                send_sem=bs_sem.at[h, side],
+                recv_sem=br_sem.at[h, side],
+                device_id=(d + step, w),
+                device_id_type=MESH,
+            )
+            for h in range(halves)
+        ]
+
+    up = boundary_copies(0, 1)
+    down = boundary_copies(1, -1)
     even = lax.rem(d, 2) == 0
-
-    @pl.when(jnp.logical_and(has_prev, even))
-    def _():
-        down.start()
-
-    @pl.when(has_next)
-    def _():
-        up.start()
-
-    @pl.when(jnp.logical_and(has_prev, jnp.logical_not(even)))
-    def _():
-        down.start()
-
-    @pl.when(jnp.logical_not(has_prev))
-    def _():
-        b_recv[0] = jnp.zeros((bnd_rows, width), BF)
-
-    @pl.when(jnp.logical_not(has_next))
-    def _():
-        b_recv[1] = jnp.zeros((bnd_rows, width), BF)
+    for h in range(halves):
+
+        @pl.when(jnp.logical_and(has_prev, even))
+        def _():
+            down[h].start()
+
+        @pl.when(has_next)
+        def _():
+            up[h].start()
+
+        @pl.when(jnp.logical_and(has_prev, jnp.logical_not(even)))
+        def _():
+            down[h].start()
+
+    for h in range(halves):
+
+        @pl.when(jnp.logical_not(has_prev))
+        def _():
+            b_recv[h, 0] = jnp.zeros((bnd_rows, half), BF)
+
+        @pl.when(jnp.logical_not(has_next))
+        def _():
+            b_recv[h, 1] = jnp.zeros((bnd_rows, half), BF)
 
     loads[2].wait()
     table_rows = node_dev + 2 * bnd_rows
@@ -207,23 +212,38 @@
     for k in range(1, fan):
         mult_t = mult_t + marks(n_rows[k : k + 1, :], node_dev)
     mult[...] = mult_t.T.reshape(peers, anch_n, node_dev)
+    loads[5].wait()
+    first = marks(pos[0:1, :], node_dev).astype(BF)
+    second = marks(pos[1:2, :], node_dev).astype(BF)
+    pairs = dot_nt(
+        jnp.concatenate([first, second], axis=1), jnp.concatenate([second, first], axis=1)
+    )
     loads[7].wait()
 
-    @pl.when(has_prev)
-    def _():
-        up.wait_recv()
-
-    @pl.when(has_next)
-    def _():
-        down.wait_recv()
-
-    received = b_recv[...].reshape(2 * bnd_rows, width)
-
-    def embedding(rows, bnd_counts, inv):
-        mean = ((own_sum[rows, :] + dot(bnd_counts, received)) * inv).astype(BF)
-        return (own_proj[rows, :] + dot(mean, wn[...])).astype(BF)
-
-    anchor_embed = embedding(pl.ds(0, n_anch), counts_a[:, node_dev:], inverse_a)
+    counts_bnd = jnp.concatenate([counts_a[:, node_dev:], counts[:, node_dev:]], axis=0)
+    inverse_both = jnp.concatenate([inverse_a, inverse], axis=0)
+
+    def projected(rows, h):
+        cols = slice(h * half, (h + 1) * half)
+        received = b_recv[h].reshape(2 * bnd_rows, half)
+        total = own_sum[rows, cols] + dot(counts_bnd[rows, :], received)
+        mean = (total * inverse_both[rows, :]).astype(BF)
+        return own_proj[rows, :] + dot(mean, wn[cols, :])
+
+    for h in range(halves):
+
+        @pl.when(has_prev)
+        def _():
+            up[h].wait_recv()
+
+        @pl.when(has_next)
+        def _():
+            down[h].wait_recv()
+
+        if h < halves - 1:
+            own_proj[...] = projected(slice(0, n_anch + node_dev), h)
+
+    anchor_embed = projected(slice(0, n_anch), halves - 1).astype(BF)
     a_send[...] = anchor_embed.reshape(peers, anch_n, width)
 
     def exchange(source, target, send, recv, to):
@@ -244,7 +264,7 @@
         copy.start()
     a_recv[pl.ds(w, 1)] = a_send[pl.ds(w, 1)]
 
-    embed = embedding(pl.ds(n_anch, node_dev), counts[:, node_dev:], inverse)
+    embed = projected(slice(n_anch, n_anch + node_dev), halves - 1).astype(BF)
     embed_v[...] = embed
     embed_t[...] = embed.T
 
@@ -256,18 +276,12 @@
         coef[v] = c
         return dot(c, embed).astype(BF)
 
+    t_recv[w] = answer(w)
     for copy, reply, v in zip(out, back, origin[1:]):
         copy.wait_recv()
         t_send[v] = answer(v)
         reply.start()
 
-    loads[5].wait()
-    first = marks(pos[0:1, :], node_dev).astype(BF)
-    second = marks(pos[1:2, :], node_dev).astype(BF)
-    pairs = dot_nt(
-        jnp.concatenate([first, second], axis=1), jnp.concatenate([second, first], axis=1)
-    )
-    t_recv[w] = answer(w)
     c_pos = pairs * (jax.nn.sigmoid(dot(embed, embed_t[...]) * scale) - 1.0)
     got = a_recv[...].reshape(n_anch, width)
     grad = dot(c_pos.astype(BF), embed) + dot_tn(coef[...].reshape(n_anch, node_dev), got)
@@ -276,13 +290,15 @@
     terms = t_recv[...].reshape(n_anch, width)
     grad_v[...] = (grad + dot(anchors_t, terms)).astype(BF)
 
-    @pl.when(has_next)
-    def _():
-        up.wait_send()
-
-    @pl.when(has_prev)
-    def _():
-        down.wait_send()
+    for h in range(halves):
+
+        @pl.when(has_next)
+        def _():
+            up[h].wait_send()
+
+        @pl.when(has_prev)
+        def _():
+            down[h].wait_send()
 
     for copy in out + back:
         copy.wait_send()
@@ -319,7 +335,7 @@
             pltpu.VMEM(w_neigh.shape, BF),
         ]
         + [pltpu.VMEM(x.shape, jnp.int32) for x in small]
-        + [pltpu.VMEM((2, bnd_rows, width), BF)] * 2
+        + [pltpu.VMEM((2, 2, bnd_rows, width // 2), BF)] * 2
         + [pltpu.VMEM(block, BF)] * 4
         + [
             pltpu.VMEM((peers, anch_n, node_dev), F32),
@@ -329,8 +345,8 @@
         + [pltpu.VMEM((peers * anch_n + node_dev, width), F32)] * 2
         + [
             pltpu.SemaphoreType.DMA((8,)),
-            pltpu.SemaphoreType.DMA((2,)),
-            pltpu.SemaphoreType.DMA((2,)),
+            pltpu.SemaphoreType.DMA((2, 2)),
+            pltpu.SemaphoreType.DMA((2, 2)),
         ]
         + [pltpu.SemaphoreType.DMA((n_wide - 1,))] * 4,
         compiler_params=pltpu.CompilerParams(

time: 15.8 us -> 15.8 us (level)
  no operation moved by 1% of the time
where the time goes in v6:
time: 15.8 us; the launch traced here: 15.6 us
  Pallas kernels  15 us (95%)
  between operations  0.64 us (4%)
    pallas_call x1, Pallas kernels, body(): pl.pallas_call(functools.partial(kernel, n_dom, n_wide), out_shape=[pltpu...  14.2 us
    pallas_call x1, Pallas kernels, body(): pl.pallas_call(store_kernel, out_shape=results, in_specs=[near] * 2, out_...  0.81 us

profile of v6, /device:TPU:9, one launch (start us, length us, event | category | flops | bytes accessed | tf_op | source)
XLA Modules:
  0.0 15.6 jit_solution(11854751747769585451)
XLA Ops:
  0.6 14.2 %shard_map.95 = (bf16[256,512]{1,0:T(8,128)(2,1)S(1)}, bf16[256,512]{1,0:T(8,128)(2,1)S(1)}) custom-call(bf16[256,512]{1,0:T(8,128)(2,1)} %feat_in.1, bf16[512,512]{1,0:T(8,128)(2,1)} %ws_in.1, bf16[512,512]{1,0:T(8,128)(2,1)} %wn_in.1, s32[1,2,64]{2,1,0:T(2,128)} %bnd_in.1, s32[16,256]{1,0:T(8,128)} %bitcast.3, s32[4,32]{1,0:T(4,128)} %anch_in.1, ...), custom_call_target="tpu_custom_call" | custom-call | tf_op jit(solution)/shard_map/pallas_call | solution.py:327
  14.8 0.8 %shard_map.96 = (bf16[256,512]{1,0:T(8,128)(2,1)}, bf16[256,512]{1,0:T(8,128)(2,1)}) custom-call(bf16[256,512]{1,0:T(8,128)(2,1)S(1)} %get-tuple-element.4.embed_v, bf16[256,512]{1,0:T(8,128)(2,1)S(1)} %get-tuple-element.5.grad_v), custom_call_target="tpu_custom_call" | custom-call | tf_op jit(solution)/shard_map/pallas_call | solution.py:356
